TPU v7x, 256 devices: a whole 4x4x8 slice. The times are simulated.
256 devices in a mesh: sx: 4 (over x_lo, core), sy: 2 (over x_hi), fsdp: 32 (over z, y).
Axes of the slice: x: 4 (x_hi: 2, x_lo: 2; x = x_hi * 2 + x_lo), y: 4, z: 8, core: 2. Of those that a mesh axis runs over, the one named last changes fastest.
Arguments:
- x_code: bfloat16 [32, 32, 32, 1536], P('fsdp', 'sx', 'sy'), may hold values from -6 to 6
- x_exp: int32 [32, 32, 32, 12], P('fsdp', 'sx', 'sy'), may hold values from -2 to 2
- dw_kernel: float32 [7, 7, 1536], replicated, may hold values from -1.2 to 1.2
- dw_bias: float32 [1536], replicated, may hold values from -4 to 4
- ln_gain: float32 [1536], replicated, may hold values from 0.1 to 1.9
- ln_bias: float32 [1536], replicated, may hold values from -3 to 3
- w_up: bfloat16 [1536, 3072], P('fsdp'), may hold values from -0.15625 to 0.15625
- b_up: float32 [3072], replicated, may hold values from -3 to 3
- w_down: bfloat16 [3072, 1536], P(None, 'fsdp'), may hold values from -0.109375 to 0.109375
- b_down: float32 [1536], replicated, may hold values from -3 to 3
- layer_scale: float32 [1536], replicated, may hold values from 0.3 to 1.5
- cotangent: bfloat16 [32, 32, 32, 1536], P('fsdp', 'sx', 'sy'), may hold values from -6 to 6
Outputs:
- block_out: bfloat16 [32, 32, 32, 1536], P('fsdp', 'sx', 'sy')
- grad_input: bfloat16 [32, 32, 32, 1536], P('fsdp', 'sx', 'sy')
- grad_kernel: float32 [7, 7, 1536], replicated
- grad_gain: float32 [1536], replicated
- grad_scale: float32 [1536], replicated
All inputs are finite; a program needn't handle non-finite values.
Results may differ from a plain program's by a relative error of at most 0.006.
Values may be sent and summed in bfloat16 or wider, within the bound.
A program may use at most 192 MiB of HBM per device.

v0:
```python
import jax
import jax.numpy as jnp
from jax import lax
from jax.sharding import PartitionSpec as P

CG = 128
KW = 7


def with_halo(shard, sides, width):
    for axis, dim in sides:
        devices, length = (lax.axis_size(axis), shard.shape[dim])
        up = [(i, (i + 1) % devices) for i in range(devices - 1)]
        down = [(j, i) for i, j in up]
        last = lax.slice_in_dim(shard, length - width, length, axis=dim)
        initial = lax.slice_in_dim(shard, 0, width, axis=dim)
        before = lax.ppermute(last, axis, up)
        after = lax.ppermute(initial, axis, down)
        shard = jnp.concatenate([before, shard, after], axis=dim)
    return shard


def gelu_tanh(v):
    return jax.nn.gelu(v, approximate=True)


def on_device(
    x_code,
    x_exp,
    dw_kernel,
    dw_bias,
    ln_gain,
    ln_bias,
    w_up,
    b_up,
    w_down,
    b_down,
    layer_scale,
    cotangent,
):
    code = x_code[0]
    rows, cols, chans = code.shape
    factor = jnp.exp2(x_exp[0].astype(jnp.float32))
    grouped = code.astype(jnp.float32).reshape(rows, cols, chans // CG, CG) * factor[..., None]
    scaled = grouped.reshape(rows, cols, chans).astype(jnp.bfloat16)
    up_full, down_full = (
        lax.all_gather(w_up, "fsdp", axis=0, tiled=True),
        lax.all_gather(w_down, "fsdp", axis=1, tiled=True),
    )
    padded_x = with_halo(scaled[None], (("sx", 1), ("sy", 2)), 3)[0].astype(jnp.float32)
    conv = jnp.zeros((rows, cols, chans), jnp.float32) + dw_bias
    for i in range(KW):
        for j in range(KW):
            conv = conv + dw_kernel[i, j] * padded_x[i : i + rows, j : j + cols]
    mean_val = jnp.mean(conv, axis=-1, keepdims=True)
    centred = conv - mean_val
    rstd = lax.rsqrt(jnp.mean(centred * centred, axis=-1, keepdims=True) + 1e-06)
    normed = centred * rstd
    ln_out = (normed * ln_gain + ln_bias).astype(jnp.bfloat16).reshape(rows * cols, chans)
    pre = jnp.dot(ln_out, up_full, preferred_element_type=jnp.float32) + b_up
    act, gelu_back = jax.vjp(gelu_tanh, pre)
    mlp = jnp.dot(act.astype(jnp.bfloat16), down_full, preferred_element_type=jnp.float32) + b_down
    mlp = mlp.reshape(rows, cols, chans)
    block_out = (scaled.astype(jnp.float32) + layer_scale * mlp).astype(jnp.bfloat16)
    grad_f = cotangent[0].astype(jnp.float32)
    scale_term = jnp.sum(grad_f * mlp, axis=(0, 1))
    d_mlp = (layer_scale * grad_f).astype(jnp.bfloat16).reshape(rows * cols, chans)
    d_act = lax.dot_general(
        d_mlp, down_full, (((1,), (1,)), ((), ())), preferred_element_type=jnp.float32
    )
    d_pre = gelu_back(d_act)[0].astype(jnp.bfloat16)
    d_ln = lax.dot_general(
        d_pre, up_full, (((1,), (1,)), ((), ())), preferred_element_type=jnp.float32
    )
    d_ln = d_ln.reshape(rows, cols, chans)
    gain_term = jnp.sum(d_ln * normed, axis=(0, 1))
    d_norm = d_ln * ln_gain
    d_conv = rstd * (
        d_norm
        - jnp.mean(d_norm, axis=-1, keepdims=True)
        - normed * jnp.mean(d_norm * normed, axis=-1, keepdims=True)
    )
    kernel_rows = []
    for i in range(KW):
        kernel_cols = []
        for j in range(KW):
            kernel_cols.append(jnp.sum(d_conv * padded_x[i : i + rows, j : j + cols], axis=(0, 1)))
        kernel_rows.append(jnp.stack(kernel_cols))
    kernel_term = jnp.stack(kernel_rows)
    padded_grad = with_halo(d_conv[None].astype(jnp.bfloat16), (("sx", 1), ("sy", 2)), 3).astype(
        jnp.float32
    )[0]
    back_conv = grad_f
    for i in range(KW):
        for j in range(KW):
            back_conv = (
                back_conv
                + dw_kernel[i, j] * padded_grad[6 - i : 6 - i + rows, 6 - j : 6 - j + cols]
            )
    grad_input = back_conv.astype(jnp.bfloat16)
    grad_kernel, grad_gain, grad_scale = lax.psum(
        (kernel_term, gain_term, scale_term), ("sx", "sy", "fsdp")
    )
    return (block_out[None], grad_input[None], grad_kernel, grad_gain, grad_scale)


def solution(mesh):
    placed = (
        P("fsdp", "sx", "sy", None),
        P("fsdp", "sx", "sy", None),
        P(),
        P(),
        P(),
        P(),
        P("fsdp", None),
        P(),
        P(None, "fsdp"),
        P(),
        P(),
        P("fsdp", "sx", "sy", None),
    )
    return jax.shard_map(
        on_device,
        mesh=mesh,
        in_specs=placed,
        out_specs=(P("fsdp", "sx", "sy", None), P("fsdp", "sx", "sy", None), P(), P(), P()),
        check_vma=False,
    )
```

profile of v0, /device:TPU:1, one launch (start us, length us, event | category | flops | bytes accessed | tf_op | source)
XLA Modules:
  0.0 522.2 jit_solution(14191568544540321584)
XLA Ops:
  7.2 0.7 all-gather.3.cloned.1.call-update
  7.9 0.7 all-gather.5.cloned.1.call-update
  8.7 0.9 exponential_bitcast_fusion
  9.6 0.1 copy.18
  9.7 0.3 mul.1066
  10.0 0.1 mul.1067
  10.3 4.5 collective-permute-start
  14.8 1.9 collective-permute-start.1
  16.8 0.3 slice_reduce_fusion.48
  17.2 0.9 slice_reduce_fusion.47
  18.3 3.0 collective-permute-done.1
  21.3 0.1 pad_maximum_fusion.3
  21.4 4.4 collective-permute-start.2
  25.8 1.3 collective-permute-start.3
  27.1 0.8 slice_reduce_fusion.46
  27.8 0.2 collective-permute-done.2
  28.1 5.4 %collective-permute-done.3 = bf16[1,14,3,1536]{3,2,1,0:T(4,128)(2,1)S(1)} collective-permute-done((bf16[1,14,3,1536]{3,2,1,0:T(4,128)(2,1)S(1)}, bf16[1,14,3,1536]{3,2,1,0:T(4,128)(2,1)S(1)}, u32[]{:S(2)}, u32[]{:S(2)}) %collective-permute-start.3) | collective-permute-done | bytes 129056 | tf_op jit(solution)/shard_map/ppermute | solution.py:18
  33.5 0.4 fusion.7
  34.2 9.4 %fusion.84 = (f32[8,16]{1,0:T(8,128)S(1)}, f32[8,16,1536]{2,1,0:T(8,128)S(1)}) fusion(f32[14,22,1536]{2,1,0:T(8,128)S(1)} %fusion.7, f32[1536]{0:T(1024)} %get-tuple-element.103, f32[1536]{0:T(1024)} %get-tuple-element.104, f32[1536]{0:T(1024)S(1)} %get-tuple-element.57, f32[1536]{0:T(1024)S(1)} %get-tuple-element.58, f32[1536]{0:T(1024)S(1)} %get-tuple-element.59, ...), kind=kLoop, calls=%fused_computation.267 | loop fusion | flops 19464064 | bytes 39629312 | tf_op jit(solution)/shard_map/reduce_sum | solution.py:55
  43.7 0.2 multiply_reduce_fusion.52
  43.9 1.7 add_convert_fusion.1
  45.6 71.9 %all-gather.3.cloned.1.call-done = bf16[1536,3072]{1,0:T(8,128)(2,1)} async-done(((bf16[48,3072]{1,0:T(8,128)(2,1)}), bf16[1536,3072]{1,0:T(8,128)(2,1)}) %all-gather.3.cloned.1.call-update) | async-done | bytes 9437200 | tf_op jit(solution)/shard_map/all_gather | solution.py:47
  117.5 6.4 %convolution_add_fusion = f32[128,3072]{1,0:T(8,128)} fusion(bf16[128,1536]{1,0:T(8,128)(2,1)} %bitcast.55, bf16[1536,3072]{1,0:T(8,128)(2,1)} %all-gather.3.cloned.1.call-done, f32[3072]{0:T(1024)S(1)} %copy-done.50), kind=kOutput, calls=%fused_computation | convolution fusion | flops 1208352768 | bytes 11415552 | tf_op jit(solution)/shard_map/dot_general | solution.py:60
  124.0 96.8 %all-gather.5.cloned.1.call-done = bf16[3072,1536]{0,1:T(8,128)(2,1)} async-done(((bf16[3072,48]{0,1:T(8,128)(2,1)}), bf16[3072,1536]{0,1:T(8,128)(2,1)}) %all-gather.5.cloned.1.call-update) | async-done | bytes 9437200 | tf_op jit(solution)/shard_map/all_gather | solution.py:48
  220.8 8.9 %fusion.61 = (f32[1536]{0:T(1024)}, bf16[128,1536]{1,0:T(8,128)(2,1)}, f32[128,1536]{1,0:T(8,128)}) fusion(bf16[1,8,16,1536]{3,2,1,0:T(8,128)(2,1)} %param.23, f32[1536]{0:T(1024)S(1)} %copy-done.51, f32[1536]{0:T(1024)S(1)} %copy-done.54, bf16[3072,1536]{0,1:T(8,128)(2,1)} %all-gather.5.cloned.1.call-done, f32[128,3072]{1,0:T(8,128)} %convolution_add_fusion), kind=kOutput, calls=%fused_computation.119 | convolution fusion | flops 1212676608 | bytes 12601344 | tf_op jit(solution)/shard_map/dot_general | solution.py:62
  229.7 13.3 %multiply_reduce_fusion.51 = (f32[128]{0:T(128)S(1)}, f32[128,1536]{1,0:T(8,128)}) fusion(f32[1536]{0:T(1024)S(1)} %copy-done.8, bf16[1536,3072]{1,0:T(8,128)(2,1)} %all-gather.3.cloned.1.call-done, f32[128,3072]{1,0:T(8,128)} %convolution_add_fusion, bf16[128,1536]{1,0:T(8,128)(2,1)} %get-tuple-element.118, ...), kind=kOutput, calls=%fused_computation.172 | convolution fusion | flops 2424176640 | bytes 21633536 | tf_op jit(solution)/shard_map/dot_general | solution.py:72
  243.0 0.1 div.17
  243.1 2.4 multiply_reduce_fusion
  245.5 2.6 multiply_reduce_fusion.1
  248.1 1.4 multiply_reduce_fusion.37
  249.6 2.0 multiply_reduce_fusion.19
  251.6 0.9 add_convert_fusion
  253.1 4.1 collective-permute-start.4
  257.2 1.9 collective-permute-start.5
  259.2 0.1 stack.217
  259.3 0.1 stack.226
  259.8 3.9 collective-permute-done.5
  263.7 0.1 fusion.83
  263.8 0.1 fusion.85
  263.9 4.3 collective-permute-start.6
  268.3 1.3 collective-permute-start.7
  269.6 0.7 copy-done.2
  270.4 75.8 %all-reduce = (f32[1536]{0:T(1024)}, f32[1536]{0:T(1024)}) all-reduce(f32[1536]{0:T(1024)S(1)} %copy-done.49, f32[1536]{0:T(1024)S(1)} %copy-done.53), channel_id=1, replica_groups=mesh['sx'=4,'sy'=2,'fsdp'=32] {'sx','sy','fsdp'}, use_global_device_ids=true, to_apply=%region_55.0 | all-reduce | flops 3072 | bytes 24576 | tf_op jit(solution)/shard_map/psum | solution.py:101
  346.3 0.6 copy-done.6
  347.0 1.4 maximum_convert_fusion
  348.4 7.7 %fusion.72 = bf16[1,8,16,1536]{3,2,1,0:T(8,128)(2,1)} fusion(f32[14,22,1536]{2,1,0:T(8,128)S(1)} %maximum_convert_fusion, f32[1536]{0:T(1024)} %get-tuple-element.103, f32[1536]{0:T(1024)} %get-tuple-element.104, f32[1536]{0:T(1024)S(1)} %get-tuple-element.57, f32[1536]{0:T(1024)S(1)} %copy-done.10, f32[1536]{0:T(1024)S(1)} %copy-done.12, ...), kind=kLoop, calls=%fused_computation.191 | loop fusion | flops 19660800 | bytes 39622656 | tf_op jit(solution)/shard_map/broadcast_in_dim | solution.py:104
  356.1 157.8 %all-reduce.3.cloned.1.call-done = f32[7,7,1536]{2,1,0:T(8,128)} async-done(((f32[7,7,1536]{2,1,0:T(8,128)}), f32[7,7,1536]{2,1,0:T(8,128)}) %all-reduce.3.cloned.1.call-update) | async-done | bytes 301072 | tf_op jit(solution)/shard_map/psum | solution.py:101
  514.0 1.7 copy.26
  (184 shorter events, 1.3 us)
Async XLA Ops:
  7.2 110.4 %all-gather.3.cloned.1.call-start = ((), (), s32[]{:S(2)}) async-start(), calls=%async_computation | async-start | bytes 9732096 | tf_op jit(solution)/shard_map/all_gather | solution.py:47
  7.9 212.9 %all-gather.5.cloned.1.call-start = ((), (), s32[]{:S(2)}) async-start(), calls=%async_computation.1 | async-start | bytes 9732096 | tf_op jit(solution)/shard_map/all_gather | solution.py:48
  8.7 505.3 %all-reduce.3.cloned.1.call-start = ((), (), s32[]{:S(2)}) async-start(), calls=%async_computation.2 | async-start | bytes 688128 | tf_op jit(solution)/shard_map/psum | solution.py:101
  10.3 8.0 %collective-permute-start = (bf16[1,3,16,1536]{3,2,1,0:T(8,128)(2,1)S(1)}, bf16[1,3,16,1536]{3,2,1,0:T(8,128)(2,1)S(1)}, u32[]{:S(2)}, u32[]{:S(2)}) collective-permute-start(bf16[1,3,16,1536]{3,2,1,0:T(8,128)(2,1)S(1)} %get-tuple-element.121), channel_id=1, source_target_pairs={{0,64},{64,128},{128,192},{1,65},{65,129},{129,193},{2,66},{66,130... | collective-permute-start | bytes 442376 | tf_op jit(solution)/shard_map/ppermute | solution.py:17
  14.8 6.5 %collective-permute-start.1 = (bf16[1,3,16,1536]{3,2,1,0:T(8,128)(2,1)S(1)}, bf16[1,3,16,1536]{3,2,1,0:T(8,128)(2,1)S(1)}, u32[]{:S(2)}, u32[]{:S(2)}) collective-permute-start(bf16[1,3,16,1536]{3,2,1,0:T(8,128)(2,1)S(1)} %get-tuple-element.122), channel_id=1, source_target_pairs={{64,0},{128,64},{192,128},{65,1},{129,65},{193,129},{66,2},{130,66... | collective-permute-start | bytes 442376 | tf_op jit(solution)/shard_map/ppermute | solution.py:18
  17.1 16.8 %copy-start.9 = (f32[1536]{0:T(1024)}, f32[1536]{0:T(1024)S(1)}, u32[]{:S(2)}) copy-start(f32[1536]{0:T(1024)S(1)} %get-tuple-element.58) | copy-start | bytes 18436
  17.1 16.8 %copy-start.11 = (f32[1536]{0:T(1024)}, f32[1536]{0:T(1024)S(1)}, u32[]{:S(2)}) copy-start(f32[1536]{0:T(1024)S(1)} %get-tuple-element.59) | copy-start | bytes 18436
  17.1 16.8 %copy-start.13 = (f32[1536]{0:T(1024)}, f32[1536]{0:T(1024)S(1)}, u32[]{:S(2)}) copy-start(f32[1536]{0:T(1024)S(1)} %get-tuple-element.60) | copy-start | bytes 18436
  17.1 16.8 %copy-start.15 = (f32[1536]{0:T(1024)}, f32[1536]{0:T(1024)S(1)}, u32[]{:S(2)}) copy-start(f32[1536]{0:T(1024)S(1)} %get-tuple-element.61) | copy-start | bytes 18436
  17.1 16.8 %copy-start.17 = (f32[1536]{0:T(1024)}, f32[1536]{0:T(1024)S(1)}, u32[]{:S(2)}) copy-start(f32[1536]{0:T(1024)S(1)} %get-tuple-element.62) | copy-start | bytes 18436
  17.1 16.8 %copy-start.19 = (f32[1536]{0:T(1024)}, f32[1536]{0:T(1024)S(1)}, u32[]{:S(2)}) copy-start(f32[1536]{0:T(1024)S(1)} %get-tuple-element.63) | copy-start | bytes 18436
  17.1 16.8 %copy-start.21 = (f32[1536]{0:T(1024)}, f32[1536]{0:T(1024)S(1)}, u32[]{:S(2)}) copy-start(f32[1536]{0:T(1024)S(1)} %get-tuple-element.64) | copy-start | bytes 18436
  17.1 16.8 %copy-start.22 = (f32[1536]{0:T(1024)}, f32[1536]{0:T(1024)S(1)}, u32[]{:S(2)}) copy-start(f32[1536]{0:T(1024)S(1)} %get-tuple-element.65) | copy-start | bytes 18436
  17.2 16.8 %copy-start.23 = (f32[1536]{0:T(1024)}, f32[1536]{0:T(1024)S(1)}, u32[]{:S(2)}) copy-start(f32[1536]{0:T(1024)S(1)} %get-tuple-element.66) | copy-start | bytes 18436
  17.2 16.8 %copy-start.24 = (f32[1536]{0:T(1024)}, f32[1536]{0:T(1024)S(1)}, u32[]{:S(2)}) copy-start(f32[1536]{0:T(1024)S(1)} %get-tuple-element.67) | copy-start | bytes 18436
  17.2 16.8 %copy-start.25 = (f32[1536]{0:T(1024)}, f32[1536]{0:T(1024)S(1)}, u32[]{:S(2)}) copy-start(f32[1536]{0:T(1024)S(1)} %get-tuple-element.68) | copy-start | bytes 18436
  17.2 16.8 %copy-start.26 = (f32[1536]{0:T(1024)}, f32[1536]{0:T(1024)S(1)}, u32[]{:S(2)}) copy-start(f32[1536]{0:T(1024)S(1)} %get-tuple-element.69) | copy-start | bytes 18436
  17.2 16.8 %copy-start.27 = (f32[1536]{0:T(1024)}, f32[1536]{0:T(1024)S(1)}, u32[]{:S(2)}) copy-start(f32[1536]{0:T(1024)S(1)} %get-tuple-element.70) | copy-start | bytes 18436
  17.2 16.8 %copy-start.28 = (f32[1536]{0:T(1024)}, f32[1536]{0:T(1024)S(1)}, u32[]{:S(2)}) copy-start(f32[1536]{0:T(1024)S(1)} %get-tuple-element.71) | copy-start | bytes 18436
  17.2 16.8 %copy-start.29 = (f32[1536]{0:T(1024)}, f32[1536]{0:T(1024)S(1)}, u32[]{:S(2)}) copy-start(f32[1536]{0:T(1024)S(1)} %get-tuple-element.72) | copy-start | bytes 18436
  17.2 16.8 %copy-start.30 = (f32[1536]{0:T(1024)}, f32[1536]{0:T(1024)S(1)}, u32[]{:S(2)}) copy-start(f32[1536]{0:T(1024)S(1)} %get-tuple-element.73) | copy-start | bytes 18436
  17.2 16.8 %copy-start.31 = (f32[1536]{0:T(1024)}, f32[1536]{0:T(1024)S(1)}, u32[]{:S(2)}) copy-start(f32[1536]{0:T(1024)S(1)} %get-tuple-element.74) | copy-start | bytes 18436
  18.2 15.9 %copy-start.37 = (f32[1536]{0:T(1024)}, f32[1536]{0:T(1024)S(1)}, u32[]{:S(2)}) copy-start(f32[1536]{0:T(1024)S(1)} %get-tuple-element.80) | copy-start | bytes 18436
  18.2 15.9 %copy-start.38 = (f32[1536]{0:T(1024)}, f32[1536]{0:T(1024)S(1)}, u32[]{:S(2)}) copy-start(f32[1536]{0:T(1024)S(1)} %get-tuple-element.81) | copy-start | bytes 18436
  18.2 15.9 %copy-start.39 = (f32[1536]{0:T(1024)}, f32[1536]{0:T(1024)S(1)}, u32[]{:S(2)}) copy-start(f32[1536]{0:T(1024)S(1)} %get-tuple-element.82) | copy-start | bytes 18436
  18.2 15.9 %copy-start.40 = (f32[1536]{0:T(1024)}, f32[1536]{0:T(1024)S(1)}, u32[]{:S(2)}) copy-start(f32[1536]{0:T(1024)S(1)} %get-tuple-element.83) | copy-start | bytes 18436
  18.2 15.9 %copy-start.41 = (f32[1536]{0:T(1024)}, f32[1536]{0:T(1024)S(1)}, u32[]{:S(2)}) copy-start(f32[1536]{0:T(1024)S(1)} %get-tuple-element.84) | copy-start | bytes 18436
  18.2 15.9 %copy-start.42 = (f32[1536]{0:T(1024)}, f32[1536]{0:T(1024)S(1)}, u32[]{:S(2)}) copy-start(f32[1536]{0:T(1024)S(1)} %get-tuple-element.85) | copy-start | bytes 18436
  18.2 15.9 %copy-start.43 = (f32[1536]{0:T(1024)}, f32[1536]{0:T(1024)S(1)}, u32[]{:S(2)}) copy-start(f32[1536]{0:T(1024)S(1)} %get-tuple-element.86) | copy-start | bytes 18436
  18.2 15.9 %copy-start.44 = (f32[1536]{0:T(1024)}, f32[1536]{0:T(1024)S(1)}, u32[]{:S(2)}) copy-start(f32[1536]{0:T(1024)S(1)} %get-tuple-element.87) | copy-start | bytes 18436
  18.3 15.9 %copy-start.45 = (f32[1536]{0:T(1024)}, f32[1536]{0:T(1024)S(1)}, u32[]{:S(2)}) copy-start(f32[1536]{0:T(1024)S(1)} %get-tuple-element.88) | copy-start | bytes 18436
  18.3 15.9 %copy-start.46 = (f32[1536]{0:T(1024)}, f32[1536]{0:T(1024)S(1)}, u32[]{:S(2)}) copy-start(f32[1536]{0:T(1024)S(1)} %get-tuple-element.89) | copy-start | bytes 18436
  21.4 6.7 %collective-permute-start.2 = (bf16[1,14,3,1536]{3,2,1,0:T(4,128)(2,1)S(1)}, bf16[1,14,3,1536]{3,2,1,0:T(4,128)(2,1)S(1)}, u32[]{:S(2)}, u32[]{:S(2)}) collective-permute-start(bf16[1,14,3,1536]{3,2,1,0:T(4,128)(2,1)S(1)} %get-tuple-element.115), channel_id=1, source_target_pairs={{0,32},{1,33},{2,34},{3,35},{4,36},{5,37},{6,38},{7,39},{8,40},{9,... | collective-permute-start | bytes 387080 | tf_op jit(solution)/shard_map/ppermute | solution.py:17
  25.8 7.7 %collective-permute-start.3 = (bf16[1,14,3,1536]{3,2,1,0:T(4,128)(2,1)S(1)}, bf16[1,14,3,1536]{3,2,1,0:T(4,128)(2,1)S(1)}, u32[]{:S(2)}, u32[]{:S(2)}) collective-permute-start(bf16[1,14,3,1536]{3,2,1,0:T(4,128)(2,1)S(1)} %get-tuple-element.116), channel_id=1, source_target_pairs={{32,0},{33,1},{34,2},{35,3},{36,4},{37,5},{38,6},{39,7},{40,8},{41... | collective-permute-start | bytes 387080 | tf_op jit(solution)/shard_map/ppermute | solution.py:18
  43.7 73.9 %copy-start.50 = (f32[3072]{0:T(1024)S(1)}, f32[3072]{0:T(1024)}, u32[]{:S(2)}) copy-start(f32[3072]{0:T(1024)} %param.19) | copy-start | bytes 36868
  117.5 103.2 %copy-start.51 = (f32[1536]{0:T(1024)S(1)}, f32[1536]{0:T(1024)}, u32[]{:S(2)}) copy-start(f32[1536]{0:T(1024)} %param.22) | copy-start | bytes 18436
  117.5 103.2 %copy-start.54 = (f32[1536]{0:T(1024)S(1)}, f32[1536]{0:T(1024)}, u32[]{:S(2)}) copy-start(f32[1536]{0:T(1024)} %param.21) | copy-start | bytes 18436
  253.1 6.7 %collective-permute-start.4 = (bf16[1,3,16,1536]{3,2,1,0:T(8,128)(2,1)S(1)}, bf16[1,3,16,1536]{3,2,1,0:T(8,128)(2,1)S(1)}, u32[]{:S(2)}, u32[]{:S(2)}) collective-permute-start(bf16[1,3,16,1536]{3,2,1,0:T(8,128)(2,1)S(1)} %get-tuple-element.119), channel_id=1, source_target_pairs={{0,64},{64,128},{128,192},{1,65},{65,129},{129,193},{2,66},{66,130... | collective-permute-start | bytes 442376 | tf_op jit(solution)/shard_map/ppermute | solution.py:17
  257.2 6.5 %collective-permute-start.5 = (bf16[1,3,16,1536]{3,2,1,0:T(8,128)(2,1)S(1)}, bf16[1,3,16,1536]{3,2,1,0:T(8,128)(2,1)S(1)}, u32[]{:S(2)}, u32[]{:S(2)}) collective-permute-start(bf16[1,3,16,1536]{3,2,1,0:T(8,128)(2,1)S(1)} %get-tuple-element.120), channel_id=1, source_target_pairs={{64,0},{128,64},{192,128},{65,1},{129,65},{193,129},{66,2},{130,66... | collective-permute-start | bytes 442376 | tf_op jit(solution)/shard_map/ppermute | solution.py:18
  263.9 82.3 %collective-permute-start.6 = (bf16[1,14,3,1536]{3,2,1,0:T(4,128)(2,1)S(1)}, bf16[1,14,3,1536]{3,2,1,0:T(4,128)(2,1)S(1)}, u32[]{:S(2)}, u32[]{:S(2)}) collective-permute-start(bf16[1,14,3,1536]{3,2,1,0:T(4,128)(2,1)S(1)} %get-tuple-element.111), channel_id=1, source_target_pairs={{0,32},{1,33},{2,34},{3,35},{4,36},{5,37},{6,38},{7,39},{8,40},{9,... | collective-permute-start | bytes 387080 | tf_op jit(solution)/shard_map/ppermute | solution.py:17
  268.3 78.0 %collective-permute-start.7 = (bf16[1,14,3,1536]{3,2,1,0:T(4,128)(2,1)S(1)}, bf16[1,14,3,1536]{3,2,1,0:T(4,128)(2,1)S(1)}, u32[]{:S(2)}, u32[]{:S(2)}) collective-permute-start(bf16[1,14,3,1536]{3,2,1,0:T(4,128)(2,1)S(1)} %get-tuple-element.112), channel_id=1, source_target_pairs={{32,0},{33,1},{34,2},{35,3},{36,4},{37,5},{38,6},{39,7},{40,8},{41... | collective-permute-start | bytes 387080 | tf_op jit(solution)/shard_map/ppermute | solution.py:18
  270.3 78.0 %copy-start.3 = (bf16[1,8,16,1536]{3,2,1,0:T(8,128)(2,1)S(1)}, bf16[1,8,16,1536]{3,2,1,0:T(8,128)(2,1)}, u32[]{:S(2)}) copy-start(bf16[1,8,16,1536]{3,2,1,0:T(8,128)(2,1)} %param.23) | copy-start | bytes 1179652
  270.3 78.0 %copy-start.10 = (f32[1536]{0:T(1024)S(1)}, f32[1536]{0:T(1024)}, u32[]{:S(2)}) copy-start(f32[1536]{0:T(1024)} %copy-done.9) | copy-start | bytes 18436
  270.3 78.0 %copy-start.12 = (f32[1536]{0:T(1024)S(1)}, f32[1536]{0:T(1024)}, u32[]{:S(2)}) copy-start(f32[1536]{0:T(1024)} %copy-done.11) | copy-start | bytes 18436
  270.4 78.0 %copy-start.14 = (f32[1536]{0:T(1024)S(1)}, f32[1536]{0:T(1024)}, u32[]{:S(2)}) copy-start(f32[1536]{0:T(1024)} %copy-done.13) | copy-start | bytes 18436
  270.4 78.0 %copy-start.16 = (f32[1536]{0:T(1024)S(1)}, f32[1536]{0:T(1024)}, u32[]{:S(2)}) copy-start(f32[1536]{0:T(1024)} %copy-done.15) | copy-start | bytes 18436
  270.4 78.0 %copy-start.18 = (f32[1536]{0:T(1024)S(1)}, f32[1536]{0:T(1024)}, u32[]{:S(2)}) copy-start(f32[1536]{0:T(1024)} %copy-done.17) | copy-start | bytes 18436
  270.4 78.0 %copy-start.20 = (f32[1536]{0:T(1024)S(1)}, f32[1536]{0:T(1024)}, u32[]{:S(2)}) copy-start(f32[1536]{0:T(1024)} %copy-done.19) | copy-start | bytes 18436
  (18 other events, 159.1 us)
Sparse Core Ops, SparseCore 0:
  10.6 106.9 all-gather.2
  120.1 100.5 all-gather.4
  270.4 243.4 all-reduce.2
where the time goes:
time: 523 us; the launch traced here: 522 us
  waiting for transfers between devices  340 us (65%)
  blocking collectives  75.8 us (14%)
  other arithmetic  31.2 us (6%)
  matrix products  28.6 us (5%)
  starting transfers between devices  23.8 us (5%)
  between operations  15.1 us (3%)
  local copies, waits for them, and re-layouts  7.13 us (1%)
    psum x1, waiting for transfers between devices, on_device(): lax.psum((kernel_term, gain_term, scale_term), ('sx', 'sy', 'fsdp'))  158 us
    all_gather x1, waiting for transfers between devices, on_device(): lax.all_gather(w_down, 'fsdp', axis=1, tiled=True)  96.8 us
    psum x1, blocking collectives, on_device(): lax.psum((kernel_term, gain_term, scale_term), ('sx', 'sy', 'fsdp'))  75.8 us
    all_gather x1, waiting for transfers between devices, on_device(): lax.all_gather(w_up, 'fsdp', axis=0, tiled=True)  71.9 us
    ppermute x4, starting transfers between devices, with_halo(): before = lax.ppermute(last, axis, up)  17.3 us
    dot_general x1, matrix products, on_device(): lax.dot_general(d_pre, up_full, (((1,), (1,)), ((), ())), preferred_eleme...  13.3 us
    ppermute x4, waiting for transfers between devices, with_halo(): after = lax.ppermute(initial, axis, down)  12.2 us
  transfers between devices with their start and end apart: 11, of which 7 were waited for; matrix products, arithmetic and copies ran while one was open for 6% of the time, Pallas kernels for 0%

commit v1 on v0

--- a/solution.py
+++ b/solution.py
@@ -45,7 +45,9 @@
     scaled = grouped.reshape(rows, cols, chans).astype(jnp.bfloat16)
     up_full, down_full = (
         lax.all_gather(w_up, "fsdp", axis=0, tiled=True),
-        lax.all_gather(w_down, "fsdp", axis=1, tiled=True),
+        jnp.concatenate(
+            lax.all_to_all(jnp.stack([w_down] * lax.axis_size("fsdp")), "fsdp", 0, 0), axis=1
+        ),
     )
     padded_x = with_halo(scaled[None], (("sx", 1), ("sy", 2)), 3)[0].astype(jnp.float32)
     conv = jnp.zeros((rows, cols, chans), jnp.float32) + dw_bias

time: 523 us -> 597 us (1.14)
  waiting for transfers between devices: 340 us -> 386 us
  starting transfers between devices: 23.8 us -> 46.4 us
  local copies, waits for them, and re-layouts: 7.13 us -> 13.5 us
    all_gather x1, waiting for transfers between devices: 71.9 us -> 211 us  [on_device(): lax.all_gather(w_up, 'fsdp', axis=0, tiled=True)]
    all_gather x1 -> x0, waiting for transfers between devices: 96.8 us -> none  [on_device(): lax.all_gather(w_down, 'fsdp', axis=1, tiled=True)]
    all_to_all x0 -> x1, starting transfers between devices: none -> 12.3 us  [on_device(): lax.all_to_all(jnp.stack([w_down] * lax.axis_size('fsdp')), 'fsdp', 0, 0)]
    ppermute x4, waiting for transfers between devices: 12.2 us -> 1.62 us  [with_halo(): after = lax.ppermute(initial, axis, down)]
    all_to_all x0 -> x1, waiting for transfers between devices: none -> 8.99 us  [on_device(): lax.all_to_all(jnp.stack([w_down] * lax.axis_size('fsdp')), 'fsdp', 0, 0)]
    ppermute x4, starting transfers between devices: 17.3 us -> 24.7 us  [with_halo(): before = lax.ppermute(last, axis, up)]
where the time goes in v1:
time: 597 us
  waiting for transfers between devices  386 us (65%)
  blocking collectives  75 us (13%)
  starting transfers between devices  46.4 us (8%)
  other arithmetic  31.4 us (5%)
  matrix products  27.9 us (5%)
  between operations  16.1 us (3%)
  local copies, waits for them, and re-layouts  13.5 us (2%)
    all_gather x1, waiting for transfers between devices, on_device(): lax.all_gather(w_up, 'fsdp', axis=0, tiled=True)  211 us
    psum x1, waiting for transfers between devices, on_device(): lax.psum((kernel_term, gain_term, scale_term), ('sx', 'sy', 'fsdp'))  161 us
    psum x1, blocking collectives, on_device(): lax.psum((kernel_term, gain_term, scale_term), ('sx', 'sy', 'fsdp'))  75 us
    ppermute x4, starting transfers between devices, with_halo(): before = lax.ppermute(last, axis, up)  24.7 us
    dot_general x1, matrix products, on_device(): lax.dot_general(d_pre, up_full, (((1,), (1,)), ((), ())), preferred_eleme...  13.4 us
    all_to_all x1, starting transfers between devices, on_device(): lax.all_to_all(jnp.stack([w_down] * lax.axis_size('fsdp')), 'fsdp', 0, 0)  12.3 us
  transfers between devices with their start and end apart: 11, of which 7 were waited for; matrix products, arithmetic and copies ran while one was open for 6% of the time, Pallas kernels for 0%

profile of v1, /device:TPU:1, one launch (start us, length us, event | category | flops | bytes accessed | tf_op | source)
XLA Modules:
  0.0 596.7 jit_solution(5169429415238454625)
XLA Ops:
  7.2 0.7 all-gather.2.cloned.1.call-update
  7.9 5.9 stack.227
  13.8 12.3 %all-to-all-start = ((bf16[32,3072,48]{1,2,0:T(8,128)(2,1)}), bf16[32,3072,48]{1,2,0:T(8,128)(2,1)}, u32[]{:S(2)}, u32[]{:S(2)}) async-start(bf16[32,3072,48]{1,2,0:T(8,128)(2,1)} %stack.227), calls=%async_computation | async-start | bytes 18874368 | tf_op jit(solution)/shard_map/all_to_all | solution.py:49
  26.2 0.1 copy.19
  26.3 0.3 mul.1065
  26.6 0.1 mul.1066
  26.8 0.3 copy-done.3
  27.2 2.9 collective-permute-start.1
  30.1 3.0 collective-permute-start
  33.1 0.3 slice_reduce_fusion.48
  33.5 0.9 slice_reduce_fusion.47
  34.6 0.6 collective-permute-done
  35.2 0.1 pad_maximum_fusion.3
  35.3 1.3 collective-permute-start.3
  36.6 5.5 collective-permute-start.2
  42.1 0.8 slice_reduce_fusion.46
  42.9 1.6 collective-permute-done.3
  44.5 1.4 collective-permute-done.2
  45.9 0.4 fusion.7
  46.6 9.4 %fusion.83 = (f32[8,16]{1,0:T(8,128)S(1)}, f32[8,16,1536]{2,1,0:T(8,128)S(1)}) fusion(f32[14,22,1536]{2,1,0:T(8,128)S(1)} %fusion.7, f32[1536]{0:T(1024)} %get-tuple-element.103, f32[1536]{0:T(1024)} %get-tuple-element.104, f32[1536]{0:T(1024)S(1)} %get-tuple-element.57, f32[1536]{0:T(1024)S(1)} %get-tuple-element.58, f32[1536]{0:T(1024)S(1)} %get-tuple-element.59, ...), kind=kLoop, calls=%fused_computation.265 | loop fusion | flops 19464064 | bytes 39629312 | tf_op jit(solution)/shard_map/reduce_sum | solution.py:57
  56.0 0.2 multiply_reduce_fusion.52
  56.3 1.7 add_convert_fusion.1
  57.9 211.2 %all-gather.2.cloned.1.call-done = bf16[1536,3072]{1,0:T(8,128)(2,1)} async-done(((bf16[48,3072]{1,0:T(8,128)(2,1)}), bf16[1536,3072]{1,0:T(8,128)(2,1)}) %all-gather.2.cloned.1.call-update) | async-done | bytes 9437200 | tf_op jit(solution)/shard_map/all_gather | solution.py:47
  269.2 6.4 %convolution_add_fusion = f32[128,3072]{1,0:T(8,128)} fusion(bf16[128,1536]{1,0:T(8,128)(2,1)} %bitcast.54, bf16[1536,3072]{1,0:T(8,128)(2,1)} %all-gather.2.cloned.1.call-done, f32[3072]{0:T(1024)S(1)} %copy-done.94), kind=kOutput, calls=%fused_computation | convolution fusion | flops 1208352768 | bytes 11415552 | tf_op jit(solution)/shard_map/dot_general | solution.py:62
  275.6 9.0 %all-to-all-done = bf16[32,3072,48]{1,2,0:T(8,128)(2,1)} async-done(((bf16[32,3072,48]{1,2,0:T(8,128)(2,1)}), bf16[32,3072,48]{1,2,0:T(8,128)(2,1)}, u32[]{:S(2)}, u32[]{:S(2)}) %all-to-all-start) | async-done | bytes 9437216 | tf_op jit(solution)/shard_map/all_to_all | solution.py:49
  284.6 8.1 %fusion.60 = (f32[1536]{0:T(1024)}, f32[128,1536]{1,0:T(8,128)S(1)}) fusion(bf16[1,8,16,1536]{3,2,1,0:T(8,128)(2,1)} %param.23, f32[1536]{0:T(1024)S(1)} %copy-done.96, bf16[3072,1536]{0,1:T(8,128)(2,1)} %bitcast.5, f32[128,3072]{1,0:T(8,128)} %convolution_add_fusion), kind=kOutput, calls=%fused_computation.116 | convolution fusion | flops 1212283392 | bytes 12201984 | tf_op jit(solution)/shard_map/dot_general | solution.py:64
  292.7 1.1 multiply_convert_fusion.2
  293.8 13.4 %multiply_reduce_fusion.51 = (f32[128]{0:T(128)S(1)}, f32[128,1536]{1,0:T(8,128)}) fusion(f32[1536]{0:T(1024)S(1)} %copy-done.7, bf16[1536,3072]{1,0:T(8,128)(2,1)} %all-gather.2.cloned.1.call-done, f32[128,3072]{1,0:T(8,128)} %convolution_add_fusion, bf16[128,1536]{1,0:T(8,128)(2,1)} %bitcast.56, bf16[3072,1536]{0,1:T(8,128)(2,1)} %bitcast.5), kind=kOutput, calls=%fused_computation.169 | convolution fusion | flops 2424176640 | bytes 21633536 | tf_op jit(solution)/shard_map/dot_general | solution.py:74
  307.1 2.3 multiply_reduce_fusion
  309.5 0.1 div.17
  309.5 4.3 multiply_reduce_fusion.1
  313.8 1.9 multiply_reduce_fusion.19
  315.9 1.4 multiply_reduce_fusion.37
  317.4 3.9 collective-permute-start.5
  321.3 10.7 %collective-permute-start.4 = (bf16[1,3,16,1536]{3,2,1,0:T(8,128)(2,1)S(1)}, bf16[1,3,16,1536]{3,2,1,0:T(8,128)(2,1)S(1)}, u32[]{:S(2)}, u32[]{:S(2)}) collective-permute-start(bf16[1,3,16,1536]{3,2,1,0:T(8,128)(2,1)S(1)} %get-tuple-element.117), channel_id=1, source_target_pairs={{0,64},{64,128},{128,192},{1,65},{65,129},{129,193},{2,66},{66,130... | collective-permute-start | bytes 442376 | tf_op jit(solution)/shard_map/ppermute | solution.py:17
  332.9 0.1 stack.253
  333.5 1.0 collective-permute-done.4
  334.5 0.1 fusion.82
  334.6 0.1 fusion.84
  334.8 1.3 collective-permute-start.7
  336.1 5.5 collective-permute-start.6
  341.6 0.7 copy-done.2
  342.8 75.0 %all-reduce = (f32[1536]{0:T(1024)}, f32[1536]{0:T(1024)}) all-reduce(f32[1536]{0:T(1024)} %get-tuple-element.54, f32[1536]{0:T(1024)} %get-tuple-element.125), channel_id=1, replica_groups=mesh['sx'=4,'sy'=2,'fsdp'=32] {'sx','sy','fsdp'}, use_global_device_ids=true, to_apply=%region_55.0 | all-reduce | flops 3072 | bytes 24576 | tf_op jit(solution)/shard_map/psum | solution.py:103
  417.8 0.7 copy-done.5
  418.5 1.4 maximum_convert_fusion
  420.3 6.9 %fusion.71 = bf16[1,8,16,1536]{3,2,1,0:T(8,128)(2,1)} fusion(f32[14,22,1536]{2,1,0:T(8,128)S(1)} %maximum_convert_fusion, f32[1536]{0:T(1024)} %get-tuple-element.103, f32[1536]{0:T(1024)} %get-tuple-element.104, f32[1536]{0:T(1024)S(1)} %get-tuple-element.57, f32[1536]{0:T(1024)S(1)} %get-tuple-element.58, f32[1536]{0:T(1024)S(1)} %get-tuple-element.59, ...), kind=kLoop, calls=%fused_computation.189 | loop fusion | flops 19660800 | bytes 39622656 | tf_op jit(solution)/shard_map/broadcast_in_dim | solution.py:106
  427.2 160.9 %all-reduce.3.cloned.1.call-done = f32[7,7,1536]{2,1,0:T(8,128)} async-done(((f32[7,7,1536]{2,1,0:T(8,128)}), f32[7,7,1536]{2,1,0:T(8,128)}) %all-reduce.3.cloned.1.call-update) | async-done | bytes 301072 | tf_op jit(solution)/shard_map/psum | solution.py:103
  588.1 1.7 copy.27
  (268 shorter events, 1.5 us)
Async XLA Ops:
  7.2 262.0 %all-gather.2.cloned.1.call-start = ((), (), s32[]{:S(2)}) async-start(), calls=%async_computation.1 | async-start | bytes 9732096 | tf_op jit(solution)/shard_map/all_gather | solution.py:47
  13.8 270.8 %all-to-all-start = ((bf16[32,3072,48]{1,2,0:T(8,128)(2,1)}), bf16[32,3072,48]{1,2,0:T(8,128)(2,1)}, u32[]{:S(2)}, u32[]{:S(2)}) async-start(bf16[32,3072,48]{1,2,0:T(8,128)(2,1)} %stack.227), calls=%async_computation | async-start | bytes 18874368 | tf_op jit(solution)/shard_map/all_to_all | solution.py:49
  26.1 562.0 %all-reduce.3.cloned.1.call-start = ((), (), s32[]{:S(2)}) async-start(), calls=%async_computation.2 | async-start | bytes 688128 | tf_op jit(solution)/shard_map/psum | solution.py:103
  27.2 7.4 %collective-permute-start.1 = (bf16[1,3,16,1536]{3,2,1,0:T(8,128)(2,1)S(1)}, bf16[1,3,16,1536]{3,2,1,0:T(8,128)(2,1)S(1)}, u32[]{:S(2)}, u32[]{:S(2)}) collective-permute-start(bf16[1,3,16,1536]{3,2,1,0:T(8,128)(2,1)S(1)} %get-tuple-element.120), channel_id=1, source_target_pairs={{64,0},{128,64},{192,128},{65,1},{129,65},{193,129},{66,2},{130,66... | collective-permute-start | bytes 442376 | tf_op jit(solution)/shard_map/ppermute | solution.py:18
  30.1 5.1 collective-permute-start
  35.3 9.2 %collective-permute-start.3 = (bf16[1,14,3,1536]{3,2,1,0:T(4,128)(2,1)S(1)}, bf16[1,14,3,1536]{3,2,1,0:T(4,128)(2,1)S(1)}, u32[]{:S(2)}, u32[]{:S(2)}) collective-permute-start(bf16[1,14,3,1536]{3,2,1,0:T(4,128)(2,1)S(1)} %get-tuple-element.116), channel_id=1, source_target_pairs={{32,0},{33,1},{34,2},{35,3},{36,4},{37,5},{38,6},{39,7},{40,8},{41... | collective-permute-start | bytes 387080 | tf_op jit(solution)/shard_map/ppermute | solution.py:18
  36.6 9.3 %collective-permute-start.2 = (bf16[1,14,3,1536]{3,2,1,0:T(4,128)(2,1)S(1)}, bf16[1,14,3,1536]{3,2,1,0:T(4,128)(2,1)S(1)}, u32[]{:S(2)}, u32[]{:S(2)}) collective-permute-start(bf16[1,14,3,1536]{3,2,1,0:T(4,128)(2,1)S(1)} %get-tuple-element.115), channel_id=1, source_target_pairs={{0,32},{1,33},{2,34},{3,35},{4,36},{5,37},{6,38},{7,39},{8,40},{9,... | collective-permute-start | bytes 387080 | tf_op jit(solution)/shard_map/ppermute | solution.py:17
  56.0 213.2 %copy-start.94 = (f32[3072]{0:T(1024)S(1)}, f32[3072]{0:T(1024)}, u32[]{:S(2)}) copy-start(f32[3072]{0:T(1024)} %param.19) | copy-start | bytes 36868
  317.4 16.1 %collective-permute-start.5 = (bf16[1,3,16,1536]{3,2,1,0:T(8,128)(2,1)S(1)}, bf16[1,3,16,1536]{3,2,1,0:T(8,128)(2,1)S(1)}, u32[]{:S(2)}, u32[]{:S(2)}) collective-permute-start(bf16[1,3,16,1536]{3,2,1,0:T(8,128)(2,1)S(1)} %get-tuple-element.118), channel_id=1, source_target_pairs={{64,0},{128,64},{192,128},{65,1},{129,65},{193,129},{66,2},{130,66... | collective-permute-start | bytes 442376 | tf_op jit(solution)/shard_map/ppermute | solution.py:18
  321.3 13.2 %collective-permute-start.4 = (bf16[1,3,16,1536]{3,2,1,0:T(8,128)(2,1)S(1)}, bf16[1,3,16,1536]{3,2,1,0:T(8,128)(2,1)S(1)}, u32[]{:S(2)}, u32[]{:S(2)}) collective-permute-start(bf16[1,3,16,1536]{3,2,1,0:T(8,128)(2,1)S(1)} %get-tuple-element.117), channel_id=1, source_target_pairs={{0,64},{64,128},{128,192},{1,65},{65,129},{129,193},{2,66},{66,130... | collective-permute-start | bytes 442376 | tf_op jit(solution)/shard_map/ppermute | solution.py:17
  334.8 83.0 %collective-permute-start.7 = (bf16[1,14,3,1536]{3,2,1,0:T(4,128)(2,1)S(1)}, bf16[1,14,3,1536]{3,2,1,0:T(4,128)(2,1)S(1)}, u32[]{:S(2)}, u32[]{:S(2)}) collective-permute-start(bf16[1,14,3,1536]{3,2,1,0:T(4,128)(2,1)S(1)} %get-tuple-element.112), channel_id=1, source_target_pairs={{32,0},{33,1},{34,2},{35,3},{36,4},{37,5},{38,6},{39,7},{40,8},{41... | collective-permute-start | bytes 387080 | tf_op jit(solution)/shard_map/ppermute | solution.py:18
  336.1 81.7 %collective-permute-start.6 = (bf16[1,14,3,1536]{3,2,1,0:T(4,128)(2,1)S(1)}, bf16[1,14,3,1536]{3,2,1,0:T(4,128)(2,1)S(1)}, u32[]{:S(2)}, u32[]{:S(2)}) collective-permute-start(bf16[1,14,3,1536]{3,2,1,0:T(4,128)(2,1)S(1)} %get-tuple-element.111), channel_id=1, source_target_pairs={{0,32},{1,33},{2,34},{3,35},{4,36},{5,37},{6,38},{7,39},{8,40},{9,... | collective-permute-start | bytes 387080 | tf_op jit(solution)/shard_map/ppermute | solution.py:17
  342.4 77.5 %copy-start.1 = (bf16[1,8,16,1536]{3,2,1,0:T(8,128)(2,1)S(1)}, bf16[1,8,16,1536]{3,2,1,0:T(8,128)(2,1)}, u32[]{:S(2)}) copy-start(bf16[1,8,16,1536]{3,2,1,0:T(8,128)(2,1)} %param.23) | copy-start | bytes 1179652
  342.4 77.5 %copy-start.9 = (f32[1536]{0:T(1024)S(1)}, f32[1536]{0:T(1024)}, u32[]{:S(2)}) copy-start(f32[1536]{0:T(1024)} %copy-done.8) | copy-start | bytes 18436
  342.4 77.5 %copy-start.11 = (f32[1536]{0:T(1024)S(1)}, f32[1536]{0:T(1024)}, u32[]{:S(2)}) copy-start(f32[1536]{0:T(1024)} %copy-done.10) | copy-start | bytes 18436
  342.4 77.5 %copy-start.13 = (f32[1536]{0:T(1024)S(1)}, f32[1536]{0:T(1024)}, u32[]{:S(2)}) copy-start(f32[1536]{0:T(1024)} %copy-done.12) | copy-start | bytes 18436
  342.4 77.5 %copy-start.15 = (f32[1536]{0:T(1024)S(1)}, f32[1536]{0:T(1024)}, u32[]{:S(2)}) copy-start(f32[1536]{0:T(1024)} %copy-done.14) | copy-start | bytes 18436
  342.4 77.5 %copy-start.17 = (f32[1536]{0:T(1024)S(1)}, f32[1536]{0:T(1024)}, u32[]{:S(2)}) copy-start(f32[1536]{0:T(1024)} %copy-done.16) | copy-start | bytes 18436
  342.4 77.5 %copy-start.19 = (f32[1536]{0:T(1024)S(1)}, f32[1536]{0:T(1024)}, u32[]{:S(2)}) copy-start(f32[1536]{0:T(1024)} %copy-done.18) | copy-start | bytes 18436
  342.4 77.5 %copy-start.21 = (f32[1536]{0:T(1024)S(1)}, f32[1536]{0:T(1024)}, u32[]{:S(2)}) copy-start(f32[1536]{0:T(1024)} %copy-done.20) | copy-start | bytes 18436
  342.5 77.5 %copy-start.23 = (f32[1536]{0:T(1024)S(1)}, f32[1536]{0:T(1024)}, u32[]{:S(2)}) copy-start(f32[1536]{0:T(1024)} %copy-done.22) | copy-start | bytes 18436
  342.5 77.5 %copy-start.25 = (f32[1536]{0:T(1024)S(1)}, f32[1536]{0:T(1024)}, u32[]{:S(2)}) copy-start(f32[1536]{0:T(1024)} %copy-done.24) | copy-start | bytes 18436
  342.5 77.5 %copy-start.27 = (f32[1536]{0:T(1024)S(1)}, f32[1536]{0:T(1024)}, u32[]{:S(2)}) copy-start(f32[1536]{0:T(1024)} %copy-done.26) | copy-start | bytes 18436
  342.5 77.5 %copy-start.29 = (f32[1536]{0:T(1024)S(1)}, f32[1536]{0:T(1024)}, u32[]{:S(2)}) copy-start(f32[1536]{0:T(1024)} %copy-done.28) | copy-start | bytes 18436
  342.5 77.5 %copy-start.31 = (f32[1536]{0:T(1024)S(1)}, f32[1536]{0:T(1024)}, u32[]{:S(2)}) copy-start(f32[1536]{0:T(1024)} %copy-done.30) | copy-start | bytes 18436
  342.5 77.5 %copy-start.33 = (f32[1536]{0:T(1024)S(1)}, f32[1536]{0:T(1024)}, u32[]{:S(2)}) copy-start(f32[1536]{0:T(1024)} %copy-done.32) | copy-start | bytes 18436
  342.5 77.5 %copy-start.35 = (f32[1536]{0:T(1024)S(1)}, f32[1536]{0:T(1024)}, u32[]{:S(2)}) copy-start(f32[1536]{0:T(1024)} %copy-done.34) | copy-start | bytes 18436
  342.5 77.5 %copy-start.37 = (f32[1536]{0:T(1024)S(1)}, f32[1536]{0:T(1024)}, u32[]{:S(2)}) copy-start(f32[1536]{0:T(1024)} %copy-done.36) | copy-start | bytes 18436
  342.5 77.5 %copy-start.39 = (f32[1536]{0:T(1024)S(1)}, f32[1536]{0:T(1024)}, u32[]{:S(2)}) copy-start(f32[1536]{0:T(1024)} %copy-done.38) | copy-start | bytes 18436
  342.5 77.5 %copy-start.41 = (f32[1536]{0:T(1024)S(1)}, f32[1536]{0:T(1024)}, u32[]{:S(2)}) copy-start(f32[1536]{0:T(1024)} %copy-done.40) | copy-start | bytes 18436
  342.6 77.5 %copy-start.43 = (f32[1536]{0:T(1024)S(1)}, f32[1536]{0:T(1024)}, u32[]{:S(2)}) copy-start(f32[1536]{0:T(1024)} %copy-done.42) | copy-start | bytes 18436
  342.6 77.5 %copy-start.45 = (f32[1536]{0:T(1024)S(1)}, f32[1536]{0:T(1024)}, u32[]{:S(2)}) copy-start(f32[1536]{0:T(1024)} %copy-done.44) | copy-start | bytes 18436
  342.6 77.5 %copy-start.47 = (f32[1536]{0:T(1024)S(1)}, f32[1536]{0:T(1024)}, u32[]{:S(2)}) copy-start(f32[1536]{0:T(1024)} %copy-done.46) | copy-start | bytes 18436
  342.6 77.5 %copy-start.49 = (f32[1536]{0:T(1024)S(1)}, f32[1536]{0:T(1024)}, u32[]{:S(2)}) copy-start(f32[1536]{0:T(1024)} %copy-done.48) | copy-start | bytes 18436
  342.6 77.5 %copy-start.51 = (f32[1536]{0:T(1024)S(1)}, f32[1536]{0:T(1024)}, u32[]{:S(2)}) copy-start(f32[1536]{0:T(1024)} %copy-done.50) | copy-start | bytes 18436
  342.6 77.5 %copy-start.53 = (f32[1536]{0:T(1024)S(1)}, f32[1536]{0:T(1024)}, u32[]{:S(2)}) copy-start(f32[1536]{0:T(1024)} %copy-done.52) | copy-start | bytes 18436
  342.6 77.5 %copy-start.55 = (f32[1536]{0:T(1024)S(1)}, f32[1536]{0:T(1024)}, u32[]{:S(2)}) copy-start(f32[1536]{0:T(1024)} %copy-done.54) | copy-start | bytes 18436
  342.6 77.5 %copy-start.57 = (f32[1536]{0:T(1024)S(1)}, f32[1536]{0:T(1024)}, u32[]{:S(2)}) copy-start(f32[1536]{0:T(1024)} %copy-done.56) | copy-start | bytes 18436
  342.6 77.5 %copy-start.59 = (f32[1536]{0:T(1024)S(1)}, f32[1536]{0:T(1024)}, u32[]{:S(2)}) copy-start(f32[1536]{0:T(1024)} %copy-done.58) | copy-start | bytes 18436
  342.6 77.5 %copy-start.61 = (f32[1536]{0:T(1024)S(1)}, f32[1536]{0:T(1024)}, u32[]{:S(2)}) copy-start(f32[1536]{0:T(1024)} %copy-done.60) | copy-start | bytes 18436
  342.7 77.5 %copy-start.63 = (f32[1536]{0:T(1024)S(1)}, f32[1536]{0:T(1024)}, u32[]{:S(2)}) copy-start(f32[1536]{0:T(1024)} %copy-done.62) | copy-start | bytes 18436
  342.7 77.5 %copy-start.64 = (f32[1536]{0:T(1024)S(1)}, f32[1536]{0:T(1024)}, u32[]{:S(2)}) copy-start(f32[1536]{0:T(1024)} %get-tuple-element.92) | copy-start | bytes 18436
  342.7 77.5 %copy-start.65 = (f32[1536]{0:T(1024)S(1)}, f32[1536]{0:T(1024)}, u32[]{:S(2)}) copy-start(f32[1536]{0:T(1024)} %get-tuple-element.93) | copy-start | bytes 18436
  342.7 77.5 %copy-start.66 = (f32[1536]{0:T(1024)S(1)}, f32[1536]{0:T(1024)}, u32[]{:S(2)}) copy-start(f32[1536]{0:T(1024)} %get-tuple-element.94) | copy-start | bytes 18436
  342.7 77.5 %copy-start.67 = (f32[1536]{0:T(1024)S(1)}, f32[1536]{0:T(1024)}, u32[]{:S(2)}) copy-start(f32[1536]{0:T(1024)} %get-tuple-element.95) | copy-start | bytes 18436
  342.7 77.5 %copy-start.68 = (f32[1536]{0:T(1024)S(1)}, f32[1536]{0:T(1024)}, u32[]{:S(2)}) copy-start(f32[1536]{0:T(1024)} %get-tuple-element.96) | copy-start | bytes 18436
  342.7 77.5 %copy-start.69 = (f32[1536]{0:T(1024)S(1)}, f32[1536]{0:T(1024)}, u32[]{:S(2)}) copy-start(f32[1536]{0:T(1024)} %get-tuple-element.97) | copy-start | bytes 18436
  342.7 77.5 %copy-start.70 = (f32[1536]{0:T(1024)S(1)}, f32[1536]{0:T(1024)}, u32[]{:S(2)}) copy-start(f32[1536]{0:T(1024)} %get-tuple-element.98) | copy-start | bytes 18436
  (60 other events, 1015.5 us)
Sparse Core Ops, SparseCore 0:
  10.6 258.5 all-gather.1
  342.5 245.5 all-reduce.2
